TPU v7x, 32 devices: a whole 2x2x4 slice. The times are simulated.
32 devices in a mesh: prow: 16 (over z, y, core), pcol: 2 (over x).
Axes of the slice: x: 2, y: 2, z: 4, core: 2. Of those that a mesh axis runs over, the one named last changes fastest.
Arguments:
- prior_panel: bfloat16 [16384, 12288], P('prow', 'pcol'), may hold values from -0.0546875 to 0.0546875
- prior_solution: bfloat16 [12288, 256], P('pcol', 'prow'), may hold values from -6 to 6
- right_side: bfloat16 [16384, 256], P('prow', 'pcol'), may hold values from -6 to 6
- new_panel: bfloat16 [2, 16384, 512], P(None, 'prow', 'pcol'), may hold values from -0.25 to 0.25
- inverses: bfloat16 [2, 512, 512], P(None, 'pcol'), as said below
Outputs:
- solved: bfloat16 [2, 512, 256], P(None, 'pcol')
- pending: float32 [16384, 256], P('prow', 'pcol')
Inputs may be any that keep to these rules, and one draw needn't show every extreme that they name: `inverses`: each of the two inverse blocks is lower triangular with a positive diagonal.
All inputs are finite; a program needn't handle non-finite values.
Results may differ from a plain program's by a relative error of at most 0.0057.
Values may be sent and summed in bfloat16 or wider, within the bound.
A program may use at most 64 MiB of HBM per device.

v0:
```python
import jax
import jax.numpy as jnp
from jax import lax
from jax.sharding import PartitionSpec as P


def spread(block, axis, owner):
    block = jnp.where(lax.axis_index(axis) == owner, block, jnp.zeros_like(block))
    return lax.psum(block, axis)


def body(prior_panel, prior_solution, right_side, new_panel, inverses):
    local_rows = prior_panel.shape[0]
    block_size = inverses.shape[2]
    pair_rows = 2 * block_size
    partial_value = jnp.dot(
        prior_panel,
        lax.all_gather(prior_solution, "prow", axis=1, tiled=True),
        preferred_element_type=jnp.float32,
    )
    row_ids = lax.axis_index("prow") * local_rows + lax.iota(jnp.int32, local_rows)
    first_panel = jnp.where(
        (row_ids >= block_size)[:, None], new_panel[0], jnp.zeros_like(new_panel[0])
    )
    second_panel = jnp.where(
        (row_ids >= pair_rows)[:, None], new_panel[1], jnp.zeros_like(new_panel[1])
    )
    pending = right_side.astype(jnp.float32) - lax.psum_scatter(
        partial_value, "pcol", scatter_dimension=1, tiled=True
    )
    solved_list = []
    for section, masked in ((0, first_panel), (1, second_panel)):
        diagonal = pending[section * block_size : (section + 1) * block_size].astype(jnp.bfloat16)
        gathered = lax.all_gather(diagonal, "pcol", axis=1, tiled=True)
        result = spread(
            jnp.dot(inverses[section], gathered, preferred_element_type=jnp.float32).astype(
                jnp.bfloat16
            ),
            "prow",
            0,
        )
        update = jnp.dot(masked, result, preferred_element_type=jnp.float32)
        pending = pending - lax.psum_scatter(update, "pcol", scatter_dimension=1, tiled=True)
        solved_list.append(result)
    first_x = solved_list[0]
    second_x = solved_list[1]
    return (jnp.stack([first_x, second_x]), pending)


def solution(mesh):
    return jax.shard_map(
        body,
        mesh=mesh,
        in_specs=(
            P("prow", "pcol"),
            P("pcol", "prow"),
            P("prow", "pcol"),
            P(None, "prow", "pcol"),
            P(None, "pcol", None),
        ),
        out_specs=(P(None, "pcol", None), P("prow", "pcol")),
        check_vma=False,
    )
```

profile of v0, /device:TPU:0, one launch (start us, length us, event | category | flops | bytes accessed | tf_op | source)
XLA Modules:
  0.0 335.1 jit_solution(1964586816087864626)
XLA Ops:
  7.2 0.0 copy-start.1
  7.2 0.0 all-gather.2.cloned.1.call-start
  7.2 0.7 all-gather.2.cloned.1.call-update
  7.9 0.0 copy-start.2
  7.9 0.0 copy-start
  7.9 0.0 reduce-scatter.4.cloned.1.call-start
  8.0 50.2 %all-gather.2.cloned.1.call-done = bf16[6144,256]{0,1:T(8,128)(2,1)} async-done(((bf16[6144,16]{0,1:T(8,128)(2,1)}), bf16[6144,256]{0,1:T(8,128)(2,1)}) %all-gather.2.cloned.1.call-update) | async-done | bytes 3145744 | tf_op jit(solution)/shard_map/all_gather | solution.py:18
  58.2 9.9 %fusion.20 = f32[1024,256]{1,0:T(8,128)} fusion(bf16[1024,6144]{1,0:T(8,128)(2,1)} %param.5, bf16[6144,256]{0,1:T(8,128)(2,1)} %all-gather.2.cloned.1.call-done), kind=kOutput, calls=%fused_computation.29 | convolution fusion | flops 3221225472 | bytes 16777216 | tf_op jit(solution)/shard_map/dot_general | solution.py:16
  68.1 0.0 reduce-scatter.4.cloned.1.call-update
  68.2 0.0 all-reduce.3.cloned.1.call-start
  68.2 19.2 %reduce-scatter.4.cloned.1.call-done = f32[1024,128]{1,0:T(8,128)} async-done(((f32[1024,256]{1,0:T(8,128)}), f32[1024,128]{1,0:T(8,128)}) %reduce-scatter.4.cloned.1.call-update) | async-done | bytes 524304 | tf_op jit(solution)/shard_map/reduce_scatter | solution.py:28
  87.4 0.0 copy-done.1
  87.4 1.1 convert_subtract_fusion
  88.5 5.9 %all_gather.10 = bf16[512,256]{1,0:T(8,128)(2,1)S(1)} all-gather(bf16[512,128]{1,0:T(8,128)(2,1)S(1)} %slice.47), channel_id=1, replica_groups=mesh['prow'=16,'pcol'=2] {'pcol'}, dimensions={1}, use_global_device_ids=true | all-gather | bytes 393216 | tf_op jit(solution)/shard_map/all_gather | solution.py:34
  94.5 0.0 copy-done.2
  94.5 0.9 fusion.1
  95.4 0.0 all-reduce.3.cloned.1.call-update
  95.4 0.0 reduce-scatter.6.cloned.1.call-start
  95.5 87.0 %all-reduce.3.cloned.1.call-done = bf16[256,256]{0,1:T(8,128)(2,1)} async-done(((bf16[256,256]{0,1:T(8,128)(2,1)}), bf16[256,256]{0,1:T(8,128)(2,1)}) %all-reduce.3.cloned.1.call-update) | async-done | bytes 131088 | tf_op jit(solution)/shard_map/psum | solution.py:9
  182.6 0.0 copy-done
  182.6 2.2 fusion.5
  184.8 0.0 reduce-scatter.6.cloned.1.call-update
  184.8 0.0 all-reduce.5.cloned.1.call-start
  184.9 22.0 %reduce-scatter.6.cloned.1.call-done = f32[1024,128]{1,0:T(8,128)} async-done(((f32[1024,256]{1,0:T(8,128)}), f32[1024,128]{1,0:T(8,128)}) %reduce-scatter.6.cloned.1.call-update) | async-done | bytes 524304 | tf_op jit(solution)/shard_map/reduce_scatter | solution.py:43
  206.9 1.1 sub.10
  208.0 6.0 %all_gather.11 = bf16[512,256]{1,0:T(8,128)(2,1)S(1)} all-gather(bf16[512,128]{1,0:T(8,128)(2,1)S(1)} %slice.46), channel_id=1, replica_groups=mesh['prow'=16,'pcol'=2] {'pcol'}, dimensions={1}, use_global_device_ids=true | all-gather | bytes 393216 | tf_op jit(solution)/shard_map/all_gather | solution.py:34
  214.0 0.9 fusion.3
  214.9 0.0 all-reduce.5.cloned.1.call-update
  215.0 0.0 reduce-scatter.8.cloned.1.call-start
  215.0 87.0 %all-reduce.5.cloned.1.call-done = bf16[256,256]{0,1:T(8,128)(2,1)} async-done(((bf16[256,256]{0,1:T(8,128)(2,1)}), bf16[256,256]{0,1:T(8,128)(2,1)}) %all-reduce.5.cloned.1.call-update) | async-done | bytes 131088 | tf_op jit(solution)/shard_map/psum | solution.py:9
  302.0 2.2 fusion.4
  304.3 0.0 reduce-scatter.8.cloned.1.call-update
  304.3 1.0 pad_maximum_fusion
  305.3 0.8 copy.7
  306.1 20.3 %reduce-scatter.8.cloned.1.call-done = f32[1024,128]{1,0:T(8,128)} async-done(((f32[1024,256]{1,0:T(8,128)}), f32[1024,128]{1,0:T(8,128)}) %reduce-scatter.8.cloned.1.call-update) | async-done | bytes 524304 | tf_op jit(solution)/shard_map/reduce_scatter | solution.py:43
  326.4 1.9 sub.11
  (4 shorter events, 0.0 us)
Async XLA Ops:
  7.2 80.3 %copy-start.1 = (bf16[1024,128]{1,0:T(8,128)(2,1)S(1)}, bf16[1024,128]{1,0:T(8,128)(2,1)}, u32[]{:S(2)}) copy-start(bf16[1024,128]{1,0:T(8,128)(2,1)} %param.7) | copy-start | bytes 786436
  7.2 51.0 %all-gather.2.cloned.1.call-start = ((), (), s32[]{:S(2)}) async-start(), calls=%async_computation.3 | async-start | bytes 3342336 | tf_op jit(solution)/shard_map/all_gather | solution.py:18
  7.9 86.6 %copy-start.2 = (bf16[2,256,512]{2,1,0:T(8,128)(2,1)S(1)}, bf16[2,256,512]{2,1,0:T(8,128)(2,1)}, u32[]{:S(2)}) copy-start(bf16[2,256,512]{2,1,0:T(8,128)(2,1)} %param.9) | copy-start | bytes 1572868
  7.9 174.6 %copy-start = (bf16[2,1024,256]{2,1,0:T(8,128)(2,1)S(1)}, bf16[2,1024,256]{2,1,0:T(8,128)(2,1)}, u32[]{:S(2)}) copy-start(bf16[2,1024,256]{2,1,0:T(8,128)(2,1)} %param.8) | copy-start | bytes 3145732
  7.9 79.5 %reduce-scatter.4.cloned.1.call-start = ((), (), s32[]{:S(2)}) async-start(), calls=%async_computation.4 | async-start | bytes 1572864 | tf_op jit(solution)/shard_map/reduce_scatter | solution.py:28
  68.2 114.4 %all-reduce.3.cloned.1.call-start = ((), (), s32[]{:S(2)}) async-start(), calls=%async_computation.5 | async-start | bytes 262144 | tf_op jit(solution)/shard_map/psum | solution.py:9
  95.4 111.5 %reduce-scatter.6.cloned.1.call-start = ((), (), s32[]{:S(2)}) async-start(), calls=%async_computation.6 | async-start | bytes 1572864 | tf_op jit(solution)/shard_map/reduce_scatter | solution.py:43
  184.8 117.2 %all-reduce.5.cloned.1.call-start = ((), (), s32[]{:S(2)}) async-start(), calls=%async_computation.7 | async-start | bytes 262144 | tf_op jit(solution)/shard_map/psum | solution.py:9
  215.0 111.4 %reduce-scatter.8.cloned.1.call-start = ((), (), s32[]{:S(2)}) async-start(), calls=%async_computation.8 | async-start | bytes 1572864 | tf_op jit(solution)/shard_map/reduce_scatter | solution.py:43
Sparse Core Ops, SparseCore 0:
  10.3 47.8 all-gather.1
  68.3 19.1 reduce-scatter.3
  95.6 86.9 all-reduce.2
  184.9 21.9 reduce-scatter.5
  215.1 86.9 all-reduce.4
  304.4 21.9 reduce-scatter.7
where the time goes:
time: 335 us
  waiting for transfers between devices  287 us (86%)
  matrix products  16.2 us (5%)
  between operations  14.2 us (4%)
  blocking collectives  11.9 us (4%)
  other arithmetic  5.08 us (2%)
    psum x2, waiting for transfers between devices, spread(): return lax.psum(block, axis)  174 us
    all_gather x1, waiting for transfers between devices, body(): lax.all_gather(prior_solution, 'prow', axis=1, tiled=True)  50.2 us
    reduce_scatter x2, waiting for transfers between devices, body(): lax.psum_scatter(update, 'pcol', scatter_dimension=1, tiled=True)  42.3 us
    reduce_scatter x1, waiting for transfers between devices, body(): lax.psum_scatter(partial_value, 'pcol', scatter_dimension=1, tiled=True)  19.2 us
    all_gather x2, blocking collectives, body(): gathered = lax.all_gather(diagonal, 'pcol', axis=1, tiled=True)  11.9 us
    dot_general x1, matrix products, body(): jnp.dot(prior_panel, lax.all_gather(prior_solution, 'prow', axis=1, tiled...  9.91 us
  transfers between devices with their start and end apart: 6, of which 6 were waited for; matrix products, arithmetic and copies ran while one was open for 1% of the time, Pallas kernels for 0%

commit v1 on v0

--- a/solution.py
+++ b/solution.py
@@ -2,6 +2,28 @@
 import jax.numpy as jnp
 from jax import lax
 from jax.sharding import PartitionSpec as P
+
+
+def in_order(blocks, dim):
+    shape = list(blocks.shape[1:])
+    shape[dim] *= blocks.shape[0]
+    return jnp.moveaxis(blocks, 0, dim).reshape(shape)
+
+
+def ring_gather(x, axis, dim):
+    count = lax.axis_size(axis)
+    pairs = [(i, (i + 1) % count) for i in range(count)]
+    back = [(b, a) for a, b in pairs]
+    lower, upper = ([], [])
+    for turn in range(count - 1):
+        if turn % 2 == 0:
+            lower.append(lax.ppermute(lower[-1] if lower else x, axis, pairs))
+        else:
+            upper.append(lax.ppermute(upper[-1] if upper else x, axis, back))
+    parts = jnp.stack([*lower[::-1], x, *upper])
+    shift = lax.axis_index(axis) - len(lower)
+    parts = parts[(jnp.arange(count) - shift) % count]
+    return in_order(parts, dim)
 
 
 def spread(block, axis, owner):
@@ -14,9 +36,7 @@
     block_size = inverses.shape[2]
     pair_rows = 2 * block_size
     partial_value = jnp.dot(
-        prior_panel,
-        lax.all_gather(prior_solution, "prow", axis=1, tiled=True),
-        preferred_element_type=jnp.float32,
+        prior_panel, ring_gather(prior_solution, "prow", 1), preferred_element_type=jnp.float32
     )
     row_ids = lax.axis_index("prow") * local_rows + lax.iota(jnp.int32, local_rows)
     first_panel = jnp.where(

time: 335 us -> 356 us (1.063)
  starting transfers between devices: 0.24 us -> 33 us
  waiting for transfers between devices: 287 us -> 265 us
  local copies, waits for them, and re-layouts: 0.89 us -> 11.1 us
    all_gather x1 -> x0, waiting for transfers between devices: 50.2 us -> none  [body(): lax.all_gather(prior_solution, 'prow', axis=1, tiled=True)]
    ppermute x0 -> x15, starting transfers between devices: none -> 32.8 us  [the longest x7 32.3 us: ring_gather(): upper.append(lax.ppermute(upper[-1] if upper else x, axis, back))]
    ppermute x0 -> x15, waiting for transfers between devices: none -> 30.5 us  [the longest x8 27.1 us: ring_gather(): lower.append(lax.ppermute(lower[-1] if lower else x, axis, pairs))]
    unnamed x7 -> x60, local copies, waits for them, and re-layouts: 0.85 us -> 8.63 us
  transfers between devices with their start and end apart: 6 -> 20, of which waited for: 6 -> 19; matrix products, arithmetic and copies ran while one was open for 1% -> 2% of each run, Pallas kernels for 0% -> 0%
where the time goes in v1:
time: 356 us; the launch traced here: 355 us
  waiting for transfers between devices  265 us (74%)
  starting transfers between devices  33 us (9%)
  matrix products  16.4 us (5%)
  between operations  14.1 us (4%)
  blocking collectives  11.8 us (3%)
  local copies, waits for them, and re-layouts  11.1 us (3%)
  other arithmetic  4.26 us (1%)
    psum x2, waiting for transfers between devices, spread(): return lax.psum(block, axis)  174 us
    reduce_scatter x2, waiting for transfers between devices, body(): lax.psum_scatter(update, 'pcol', scatter_dimension=1, tiled=True)  42.3 us
    ppermute x7, starting transfers between devices, ring_gather(): upper.append(lax.ppermute(upper[-1] if upper else x, axis, back))  32.3 us
    ppermute x8, waiting for transfers between devices, ring_gather(): lower.append(lax.ppermute(lower[-1] if lower else x, axis, pairs))  27.1 us
    reduce_scatter x1, waiting for transfers between devices, body(): lax.psum_scatter(partial_value, 'pcol', scatter_dimension=1, tiled=True)  17.9 us
    all_gather x2, blocking collectives, body(): gathered = lax.all_gather(diagonal, 'pcol', axis=1, tiled=True)  11.8 us
    dot_general x1, matrix products, body(): jnp.dot(prior_panel, ring_gather(prior_solution, 'prow', 1), preferred_el...  9.98 us
    unnamed x60, local copies, waits for them, and re-layouts  8.63 us
  transfers between devices with their start and end apart: 20, of which 19 were waited for; matrix products, arithmetic and copies ran while one was open for 2% of the time, Pallas kernels for 0%

profile of v1, /device:TPU:0, one launch (start us, length us, event | category | flops | bytes accessed | tf_op | source)
XLA Modules:
  0.0 355.5 jit_solution(15886191368487538575)
XLA Ops:
  7.2 0.5 collective-permute-start
  7.7 8.6 %collective-permute-done = bf16[6144,16]{0,1:T(8,128)(2,1)S(1)} collective-permute-done((bf16[6144,16]{0,1:T(8,128)(2,1)}, bf16[6144,16]{0,1:T(8,128)(2,1)S(1)}, u32[]{:S(2)}, u32[]{:S(2)}) %collective-permute-start) | collective-permute-done | bytes 196640 | tf_op jit(solution)/shard_map/ppermute | solution.py:20
  16.3 4.4 %collective-permute-start.8 = (bf16[6144,16]{0,1:T(8,128)(2,1)}, bf16[6144,16]{0,1:T(8,128)(2,1)S(1)}, u32[]{:S(2)}, u32[]{:S(2)}) collective-permute-start(bf16[6144,16]{0,1:T(8,128)(2,1)} %param.6), channel_id=1, source_target_pairs={{2,0},{4,2},{6,4},{8,6},{10,8},{12,10},{14,12},{16,14},{18,16},{20... | collective-permute-start | bytes 589832 | tf_op jit(solution)/shard_map/ppermute | solution.py:22
  20.7 3.3 collective-permute-done.1
  24.1 0.1 collective-permute-done.8
  24.2 0.7 copy-done.4
  24.9 4.6 %collective-permute-start.9 = (bf16[6144,16]{0,1:T(8,128)(2,1)S(1)}, bf16[6144,16]{0,1:T(8,128)(2,1)S(1)}, u32[]{:S(2)}, u32[]{:S(2)}) collective-permute-start(bf16[6144,16]{0,1:T(8,128)(2,1)S(1)} %collective-permute-done.8), channel_id=1, source_target_pairs={{2,0},{4,2},{6,4},{8,6},{10,8},{12,10},{14,12},{16,14},{18,16},{20... | collective-permute-start | bytes 589832 | tf_op jit(solution)/shard_map/ppermute | solution.py:22
  29.5 2.5 collective-permute-done.2
  32.0 0.7 collective-permute-done.9
  32.7 4.7 %collective-permute-start.10 = (bf16[6144,16]{0,1:T(8,128)(2,1)S(1)}, bf16[6144,16]{0,1:T(8,128)(2,1)S(1)}, u32[]{:S(2)}, u32[]{:S(2)}) collective-permute-start(bf16[6144,16]{0,1:T(8,128)(2,1)S(1)} %collective-permute-done.9), channel_id=1, source_target_pairs={{2,0},{4,2},{6,4},{8,6},{10,8},{12,10},{14,12},{16,14},{18,16},{20... | collective-permute-start | bytes 589832 | tf_op jit(solution)/shard_map/ppermute | solution.py:22
  37.4 2.5 collective-permute-done.3
  39.9 0.7 collective-permute-done.10
  40.6 4.6 %collective-permute-start.11 = (bf16[6144,16]{0,1:T(8,128)(2,1)S(1)}, bf16[6144,16]{0,1:T(8,128)(2,1)S(1)}, u32[]{:S(2)}, u32[]{:S(2)}) collective-permute-start(bf16[6144,16]{0,1:T(8,128)(2,1)S(1)} %collective-permute-done.10), channel_id=1, source_target_pairs={{2,0},{4,2},{6,4},{8,6},{10,8},{12,10},{14,12},{16,14},{18,16},{20... | collective-permute-start | bytes 589832 | tf_op jit(solution)/shard_map/ppermute | solution.py:22
  45.2 2.6 collective-permute-done.4
  47.8 0.6 collective-permute-done.11
  48.5 4.6 %collective-permute-start.12 = (bf16[6144,16]{0,1:T(8,128)(2,1)S(1)}, bf16[6144,16]{0,1:T(8,128)(2,1)S(1)}, u32[]{:S(2)}, u32[]{:S(2)}) collective-permute-start(bf16[6144,16]{0,1:T(8,128)(2,1)S(1)} %collective-permute-done.11), channel_id=1, source_target_pairs={{2,0},{4,2},{6,4},{8,6},{10,8},{12,10},{14,12},{16,14},{18,16},{20... | collective-permute-start | bytes 589832 | tf_op jit(solution)/shard_map/ppermute | solution.py:22
  53.1 2.6 collective-permute-done.5
  55.7 0.6 collective-permute-done.12
  56.3 4.7 %collective-permute-start.13 = (bf16[6144,16]{0,1:T(8,128)(2,1)S(1)}, bf16[6144,16]{0,1:T(8,128)(2,1)S(1)}, u32[]{:S(2)}, u32[]{:S(2)}) collective-permute-start(bf16[6144,16]{0,1:T(8,128)(2,1)S(1)} %collective-permute-done.12), channel_id=1, source_target_pairs={{2,0},{4,2},{6,4},{8,6},{10,8},{12,10},{14,12},{16,14},{18,16},{20... | collective-permute-start | bytes 589832 | tf_op jit(solution)/shard_map/ppermute | solution.py:22
  61.0 2.6 collective-permute-done.6
  63.6 0.6 collective-permute-done.13
  64.2 4.6 %collective-permute-start.14 = (bf16[6144,16]{0,1:T(8,128)(2,1)S(1)}, bf16[6144,16]{0,1:T(8,128)(2,1)S(1)}, u32[]{:S(2)}, u32[]{:S(2)}) collective-permute-start(bf16[6144,16]{0,1:T(8,128)(2,1)S(1)} %collective-permute-done.13), channel_id=1, source_target_pairs={{2,0},{4,2},{6,4},{8,6},{10,8},{12,10},{14,12},{16,14},{18,16},{20... | collective-permute-start | bytes 589832 | tf_op jit(solution)/shard_map/ppermute | solution.py:22
  68.8 2.5 collective-permute-done.7
  71.4 1.0 bitcast_dynamic-update-slice_fusion.14
  72.4 0.9 bitcast_dynamic-update-slice_fusion.13
  73.3 0.9 bitcast_dynamic-update-slice_fusion.12
  74.3 0.9 bitcast_dynamic-update-slice_fusion.11
  75.2 0.9 bitcast_dynamic-update-slice_fusion.10
  76.2 0.9 bitcast_dynamic-update-slice_fusion.9
  77.4 2.4 gather_fusion
  79.8 10.0 %convolution_bitcast_fusion = f32[1024,256]{0,1:T(8,128)} fusion(bf16[6144,256]{0,1:T(8,128)(2,1)} %bitcast.63, bf16[1024,6144]{1,0:T(8,128)(2,1)} %param.5), kind=kOutput, calls=%fused_computation.1 | convolution fusion | flops 3221225472 | bytes 16777216 | tf_op jit(solution)/shard_map/dot_general | solution.py:38
  90.0 17.9 %reduce-scatter.4.cloned.1.call-done = f32[1024,128]{0,1:T(8,128)} async-done(((f32[1024,256]{0,1:T(8,128)}), f32[1024,128]{0,1:T(8,128)}) %reduce-scatter.4.cloned.1.call-update) | async-done | bytes 524304 | tf_op jit(solution)/shard_map/reduce_scatter | solution.py:48
  107.9 1.1 convert_subtract_fusion
  109.1 5.9 %all_gather.6 = bf16[512,256]{0,1:T(8,128)(2,1)S(1)} all-gather(bf16[512,128]{0,1:T(8,128)(2,1)S(1)} %slice.49), channel_id=1, replica_groups=mesh['prow'=16,'pcol'=2] {'pcol'}, dimensions={1}, use_global_device_ids=true | all-gather | bytes 393216 | tf_op jit(solution)/shard_map/all_gather | solution.py:54
  115.0 0.9 fusion.1
  116.0 87.0 %all-reduce.3.cloned.1.call-done = bf16[256,256]{0,1:T(8,128)(2,1)} async-done(((bf16[256,256]{0,1:T(8,128)(2,1)}), bf16[256,256]{0,1:T(8,128)(2,1)}) %all-reduce.3.cloned.1.call-update) | async-done | bytes 131088 | tf_op jit(solution)/shard_map/psum | solution.py:31
  203.0 2.3 fusion.5
  205.4 22.0 %reduce-scatter.6.cloned.1.call-done = f32[1024,128]{0,1:T(8,128)} async-done(((f32[1024,256]{0,1:T(8,128)}), f32[1024,128]{0,1:T(8,128)}) %reduce-scatter.6.cloned.1.call-update) | async-done | bytes 524304 | tf_op jit(solution)/shard_map/reduce_scatter | solution.py:63
  227.4 1.1 sub.29
  228.5 5.9 %all_gather.7 = bf16[512,256]{0,1:T(8,128)(2,1)S(1)} all-gather(bf16[512,128]{0,1:T(8,128)(2,1)S(1)} %slice.48), channel_id=1, replica_groups=mesh['prow'=16,'pcol'=2] {'pcol'}, dimensions={1}, use_global_device_ids=true | all-gather | bytes 393216 | tf_op jit(solution)/shard_map/all_gather | solution.py:54
  234.4 0.9 fusion.3
  235.5 87.0 %all-reduce.5.cloned.1.call-done = bf16[256,256]{0,1:T(8,128)(2,1)} async-done(((bf16[256,256]{0,1:T(8,128)(2,1)}), bf16[256,256]{0,1:T(8,128)(2,1)}) %all-reduce.5.cloned.1.call-update) | async-done | bytes 131088 | tf_op jit(solution)/shard_map/psum | solution.py:31
  322.4 2.3 fusion.4
  324.8 0.9 pad_maximum_fusion
  325.7 0.8 copy.10
  326.5 20.3 %reduce-scatter.8.cloned.1.call-done = f32[1024,128]{0,1:T(8,128)} async-done(((f32[1024,256]{0,1:T(8,128)}), f32[1024,128]{0,1:T(8,128)}) %reduce-scatter.8.cloned.1.call-update) | async-done | bytes 524304 | tf_op jit(solution)/shard_map/reduce_scatter | solution.py:63
  346.9 1.1 sub.30
  348.0 1.0 copy.11
  (76 shorter events, 0.8 us)
Async XLA Ops:
  7.2 70.0 %copy-start.3 = (bf16[6144,16]{0,1:T(8,128)(2,1)S(1)}, bf16[6144,16]{0,1:T(8,128)(2,1)}, u32[]{:S(2)}) copy-start(bf16[6144,16]{0,1:T(8,128)(2,1)} %param.6) | copy-start | bytes 589828
  7.2 100.8 %reduce-scatter.4.cloned.1.call-start = ((), (), s32[]{:S(2)}) async-start(), calls=%async_computation.3 | async-start | bytes 1572864 | tf_op jit(solution)/shard_map/reduce_scatter | solution.py:48
  7.2 9.1 %collective-permute-start = (bf16[6144,16]{0,1:T(8,128)(2,1)}, bf16[6144,16]{0,1:T(8,128)(2,1)S(1)}, u32[]{:S(2)}, u32[]{:S(2)}) collective-permute-start(bf16[6144,16]{0,1:T(8,128)(2,1)} %param.6), channel_id=1, source_target_pairs={{0,2},{2,4},{4,6},{6,8},{8,10},{10,12},{12,14},{14,16},{16,18},{18... | collective-permute-start | bytes 589832 | tf_op jit(solution)/shard_map/ppermute | solution.py:20
  16.3 7.8 %collective-permute-start.1 = (bf16[6144,16]{0,1:T(8,128)(2,1)S(1)}, bf16[6144,16]{0,1:T(8,128)(2,1)S(1)}, u32[]{:S(2)}, u32[]{:S(2)}) collective-permute-start(bf16[6144,16]{0,1:T(8,128)(2,1)S(1)} %collective-permute-done), channel_id=1, source_target_pairs={{0,2},{2,4},{4,6},{6,8},{8,10},{10,12},{12,14},{14,16},{16,18},{18... | collective-permute-start | bytes 589832 | tf_op jit(solution)/shard_map/ppermute | solution.py:20
  16.3 7.9 %collective-permute-start.8 = (bf16[6144,16]{0,1:T(8,128)(2,1)}, bf16[6144,16]{0,1:T(8,128)(2,1)S(1)}, u32[]{:S(2)}, u32[]{:S(2)}) collective-permute-start(bf16[6144,16]{0,1:T(8,128)(2,1)} %param.6), channel_id=1, source_target_pairs={{2,0},{4,2},{6,4},{8,6},{10,8},{12,10},{14,12},{16,14},{18,16},{20... | collective-permute-start | bytes 589832 | tf_op jit(solution)/shard_map/ppermute | solution.py:22
  24.1 8.6 %copy-start.6 = (bf16[6144,16]{0,1:T(8,128)(2,1)}, bf16[6144,16]{0,1:T(8,128)(2,1)S(1)}, u32[]{:S(2)}) copy-start(bf16[6144,16]{0,1:T(8,128)(2,1)S(1)} %collective-permute-done.1) | copy-start | bytes 589828
  24.1 7.9 %collective-permute-start.2 = (bf16[6144,16]{0,1:T(8,128)(2,1)S(1)}, bf16[6144,16]{0,1:T(8,128)(2,1)S(1)}, u32[]{:S(2)}, u32[]{:S(2)}) collective-permute-start(bf16[6144,16]{0,1:T(8,128)(2,1)S(1)} %collective-permute-done.1), channel_id=1, source_target_pairs={{0,2},{2,4},{4,6},{6,8},{8,10},{10,12},{12,14},{14,16},{16,18},{18... | collective-permute-start | bytes 589832 | tf_op jit(solution)/shard_map/ppermute | solution.py:20
  24.2 0.7 copy-start.4
  24.9 7.8 %collective-permute-start.9 = (bf16[6144,16]{0,1:T(8,128)(2,1)S(1)}, bf16[6144,16]{0,1:T(8,128)(2,1)S(1)}, u32[]{:S(2)}, u32[]{:S(2)}) collective-permute-start(bf16[6144,16]{0,1:T(8,128)(2,1)S(1)} %collective-permute-done.8), channel_id=1, source_target_pairs={{2,0},{4,2},{6,4},{8,6},{10,8},{12,10},{14,12},{16,14},{18,16},{20... | collective-permute-start | bytes 589832 | tf_op jit(solution)/shard_map/ppermute | solution.py:22
  32.0 8.6 %copy-start.9 = (bf16[6144,16]{0,1:T(8,128)(2,1)}, bf16[6144,16]{0,1:T(8,128)(2,1)S(1)}, u32[]{:S(2)}) copy-start(bf16[6144,16]{0,1:T(8,128)(2,1)S(1)} %collective-permute-done.2) | copy-start | bytes 589828
  32.0 7.9 %collective-permute-start.3 = (bf16[6144,16]{0,1:T(8,128)(2,1)S(1)}, bf16[6144,16]{0,1:T(8,128)(2,1)S(1)}, u32[]{:S(2)}, u32[]{:S(2)}) collective-permute-start(bf16[6144,16]{0,1:T(8,128)(2,1)S(1)} %collective-permute-done.2), channel_id=1, source_target_pairs={{0,2},{2,4},{4,6},{6,8},{8,10},{10,12},{12,14},{14,16},{16,18},{18... | collective-permute-start | bytes 589832 | tf_op jit(solution)/shard_map/ppermute | solution.py:20
  32.7 4.7 %copy-start.7 = (bf16[6144,16]{0,1:T(8,128)(2,1)}, bf16[6144,16]{0,1:T(8,128)(2,1)S(1)}, u32[]{:S(2)}) copy-start(bf16[6144,16]{0,1:T(8,128)(2,1)S(1)} %collective-permute-done.9) | copy-start | bytes 589828
  32.7 7.9 %collective-permute-start.10 = (bf16[6144,16]{0,1:T(8,128)(2,1)S(1)}, bf16[6144,16]{0,1:T(8,128)(2,1)S(1)}, u32[]{:S(2)}, u32[]{:S(2)}) collective-permute-start(bf16[6144,16]{0,1:T(8,128)(2,1)S(1)} %collective-permute-done.9), channel_id=1, source_target_pairs={{2,0},{4,2},{6,4},{8,6},{10,8},{12,10},{14,12},{16,14},{18,16},{20... | collective-permute-start | bytes 589832 | tf_op jit(solution)/shard_map/ppermute | solution.py:22
  39.9 28.9 %copy-start.14 = (bf16[6144,16]{0,1:T(8,128)(2,1)}, bf16[6144,16]{0,1:T(8,128)(2,1)S(1)}, u32[]{:S(2)}) copy-start(bf16[6144,16]{0,1:T(8,128)(2,1)S(1)} %collective-permute-done.3) | copy-start | bytes 589828
  39.9 7.9 %collective-permute-start.4 = (bf16[6144,16]{0,1:T(8,128)(2,1)S(1)}, bf16[6144,16]{0,1:T(8,128)(2,1)S(1)}, u32[]{:S(2)}, u32[]{:S(2)}) collective-permute-start(bf16[6144,16]{0,1:T(8,128)(2,1)S(1)} %collective-permute-done.3), channel_id=1, source_target_pairs={{0,2},{2,4},{4,6},{6,8},{8,10},{10,12},{12,14},{14,16},{16,18},{18... | collective-permute-start | bytes 589832 | tf_op jit(solution)/shard_map/ppermute | solution.py:20
  40.6 4.6 %copy-start.10 = (bf16[6144,16]{0,1:T(8,128)(2,1)}, bf16[6144,16]{0,1:T(8,128)(2,1)S(1)}, u32[]{:S(2)}) copy-start(bf16[6144,16]{0,1:T(8,128)(2,1)S(1)} %collective-permute-done.10) | copy-start | bytes 589828
  40.6 7.8 %collective-permute-start.11 = (bf16[6144,16]{0,1:T(8,128)(2,1)S(1)}, bf16[6144,16]{0,1:T(8,128)(2,1)S(1)}, u32[]{:S(2)}, u32[]{:S(2)}) collective-permute-start(bf16[6144,16]{0,1:T(8,128)(2,1)S(1)} %collective-permute-done.10), channel_id=1, source_target_pairs={{2,0},{4,2},{6,4},{8,6},{10,8},{12,10},{14,12},{16,14},{18,16},{20... | collective-permute-start | bytes 589832 | tf_op jit(solution)/shard_map/ppermute | solution.py:22
  47.8 0.7 copy-start.17
  47.8 7.9 %collective-permute-start.5 = (bf16[6144,16]{0,1:T(8,128)(2,1)S(1)}, bf16[6144,16]{0,1:T(8,128)(2,1)S(1)}, u32[]{:S(2)}, u32[]{:S(2)}) collective-permute-start(bf16[6144,16]{0,1:T(8,128)(2,1)S(1)} %collective-permute-done.4), channel_id=1, source_target_pairs={{0,2},{2,4},{4,6},{6,8},{8,10},{10,12},{12,14},{14,16},{16,18},{18... | collective-permute-start | bytes 589832 | tf_op jit(solution)/shard_map/ppermute | solution.py:20
  48.5 20.3 %copy-start.12 = (bf16[6144,16]{0,1:T(8,128)(2,1)}, bf16[6144,16]{0,1:T(8,128)(2,1)S(1)}, u32[]{:S(2)}) copy-start(bf16[6144,16]{0,1:T(8,128)(2,1)S(1)} %collective-permute-done.11) | copy-start | bytes 589828
  48.5 7.8 %collective-permute-start.12 = (bf16[6144,16]{0,1:T(8,128)(2,1)S(1)}, bf16[6144,16]{0,1:T(8,128)(2,1)S(1)}, u32[]{:S(2)}, u32[]{:S(2)}) collective-permute-start(bf16[6144,16]{0,1:T(8,128)(2,1)S(1)} %collective-permute-done.11), channel_id=1, source_target_pairs={{2,0},{4,2},{6,4},{8,6},{10,8},{12,10},{14,12},{16,14},{18,16},{20... | collective-permute-start | bytes 589832 | tf_op jit(solution)/shard_map/ppermute | solution.py:22
  55.7 13.1 %copy-start.18 = (bf16[6144,16]{0,1:T(8,128)(2,1)}, bf16[6144,16]{0,1:T(8,128)(2,1)S(1)}, u32[]{:S(2)}) copy-start(bf16[6144,16]{0,1:T(8,128)(2,1)S(1)} %collective-permute-done.5) | copy-start | bytes 589828
  55.7 7.9 %collective-permute-start.6 = (bf16[6144,16]{0,1:T(8,128)(2,1)S(1)}, bf16[6144,16]{0,1:T(8,128)(2,1)S(1)}, u32[]{:S(2)}, u32[]{:S(2)}) collective-permute-start(bf16[6144,16]{0,1:T(8,128)(2,1)S(1)} %collective-permute-done.5), channel_id=1, source_target_pairs={{0,2},{2,4},{4,6},{6,8},{8,10},{10,12},{12,14},{14,16},{16,18},{18... | collective-permute-start | bytes 589832 | tf_op jit(solution)/shard_map/ppermute | solution.py:20
  55.7 21.5 %copy-start.5 = (bf16[6144,16]{0,1:T(8,128)(2,1)S(1)}, bf16[6144,16]{0,1:T(8,128)(2,1)}, u32[]{:S(2)}) copy-start(bf16[6144,16]{0,1:T(8,128)(2,1)} %copy-done.4) | copy-start | bytes 589828
  55.7 21.5 %copy-start.8 = (bf16[6144,16]{0,1:T(8,128)(2,1)S(1)}, bf16[6144,16]{0,1:T(8,128)(2,1)}, u32[]{:S(2)}) copy-start(bf16[6144,16]{0,1:T(8,128)(2,1)} %copy-done.7) | copy-start | bytes 589828
  55.7 21.5 %copy-start.11 = (bf16[6144,16]{0,1:T(8,128)(2,1)S(1)}, bf16[6144,16]{0,1:T(8,128)(2,1)}, u32[]{:S(2)}) copy-start(bf16[6144,16]{0,1:T(8,128)(2,1)} %copy-done.10) | copy-start | bytes 589828
  56.3 12.5 %copy-start.15 = (bf16[6144,16]{0,1:T(8,128)(2,1)}, bf16[6144,16]{0,1:T(8,128)(2,1)S(1)}, u32[]{:S(2)}) copy-start(bf16[6144,16]{0,1:T(8,128)(2,1)S(1)} %collective-permute-done.12) | copy-start | bytes 589828
  56.3 7.9 %collective-permute-start.13 = (bf16[6144,16]{0,1:T(8,128)(2,1)S(1)}, bf16[6144,16]{0,1:T(8,128)(2,1)S(1)}, u32[]{:S(2)}, u32[]{:S(2)}) collective-permute-start(bf16[6144,16]{0,1:T(8,128)(2,1)S(1)} %collective-permute-done.12), channel_id=1, source_target_pairs={{2,0},{4,2},{6,4},{8,6},{10,8},{12,10},{14,12},{16,14},{18,16},{20... | collective-permute-start | bytes 589832 | tf_op jit(solution)/shard_map/ppermute | solution.py:22
  63.6 5.2 %copy-start.19 = (bf16[6144,16]{0,1:T(8,128)(2,1)}, bf16[6144,16]{0,1:T(8,128)(2,1)S(1)}, u32[]{:S(2)}) copy-start(bf16[6144,16]{0,1:T(8,128)(2,1)S(1)} %collective-permute-done.6) | copy-start | bytes 589828
  63.6 7.8 %collective-permute-start.7 = (bf16[6144,16]{0,1:T(8,128)(2,1)S(1)}, bf16[6144,16]{0,1:T(8,128)(2,1)S(1)}, u32[]{:S(2)}, u32[]{:S(2)}) collective-permute-start(bf16[6144,16]{0,1:T(8,128)(2,1)S(1)} %collective-permute-done.6), channel_id=1, source_target_pairs={{0,2},{2,4},{4,6},{6,8},{8,10},{10,12},{12,14},{14,16},{16,18},{18... | collective-permute-start | bytes 589832 | tf_op jit(solution)/shard_map/ppermute | solution.py:20
  64.2 13.2 %collective-permute-start.14 = (bf16[6144,16]{0,1:T(8,128)(2,1)S(1)}, bf16[6144,16]{0,1:T(8,128)(2,1)S(1)}, u32[]{:S(2)}, u32[]{:S(2)}) collective-permute-start(bf16[6144,16]{0,1:T(8,128)(2,1)S(1)} %collective-permute-done.13), channel_id=1, source_target_pairs={{2,0},{4,2},{6,4},{8,6},{10,8},{12,10},{14,12},{16,14},{18,16},{20... | collective-permute-start | bytes 589832 | tf_op jit(solution)/shard_map/ppermute | solution.py:22
  71.4 5.9 %copy-start.13 = (bf16[6144,16]{0,1:T(8,128)(2,1)S(1)}, bf16[6144,16]{0,1:T(8,128)(2,1)}, u32[]{:S(2)}) copy-start(bf16[6144,16]{0,1:T(8,128)(2,1)} %copy-done.12) | copy-start | bytes 589828
  71.4 5.9 %copy-start.16 = (bf16[6144,16]{0,1:T(8,128)(2,1)S(1)}, bf16[6144,16]{0,1:T(8,128)(2,1)}, u32[]{:S(2)}) copy-start(bf16[6144,16]{0,1:T(8,128)(2,1)} %copy-done.15) | copy-start | bytes 589828
  79.8 10.1 %copy-start.2 = (bf16[1024,128]{1,0:T(8,128)(2,1)S(1)}, bf16[1024,128]{1,0:T(8,128)(2,1)}, u32[]{:S(2)}) copy-start(bf16[1024,128]{1,0:T(8,128)(2,1)} %param.7) | copy-start | bytes 786436
  89.8 25.2 %copy-start.20 = (bf16[2,256,512]{2,1,0:T(8,128)(2,1)S(1)}, bf16[2,256,512]{2,1,0:T(8,128)(2,1)}, u32[]{:S(2)}) copy-start(bf16[2,256,512]{2,1,0:T(8,128)(2,1)} %param.9) | copy-start | bytes 1572868
  89.8 113.2 %copy-start = (bf16[2,1024,256]{2,1,0:T(8,128)(2,1)S(1)}, bf16[2,1024,256]{2,1,0:T(8,128)(2,1)}, u32[]{:S(2)}) copy-start(bf16[2,1024,256]{2,1,0:T(8,128)(2,1)} %param.8) | copy-start | bytes 3145732
  89.8 113.2 %all-reduce.3.cloned.1.call-start = ((), (), s32[]{:S(2)}) async-start(), calls=%async_computation.4 | async-start | bytes 262144 | tf_op jit(solution)/shard_map/psum | solution.py:31
  115.9 111.5 %reduce-scatter.6.cloned.1.call-start = ((), (), s32[]{:S(2)}) async-start(), calls=%async_computation.5 | async-start | bytes 1572864 | tf_op jit(solution)/shard_map/reduce_scatter | solution.py:63
  205.3 119.5 %copy-start.1 = (bf16[256,256]{0,1:T(8,128)(2,1)S(1)}, bf16[256,256]{0,1:T(8,128)(2,1)}, u32[]{:S(2)}) copy-start(bf16[256,256]{0,1:T(8,128)(2,1)} %all-reduce.3.cloned.1.call-done) | copy-start | bytes 393220
  205.3 117.1 %all-reduce.5.cloned.1.call-start = ((), (), s32[]{:S(2)}) async-start(), calls=%async_computation.6 | async-start | bytes 262144 | tf_op jit(solution)/shard_map/psum | solution.py:31
  235.4 111.5 %reduce-scatter.8.cloned.1.call-start = ((), (), s32[]{:S(2)}) async-start(), calls=%async_computation.7 | async-start | bytes 1572864 | tf_op jit(solution)/shard_map/reduce_scatter | solution.py:63
Sparse Core Ops, SparseCore 0:
  89.9 17.9 reduce-scatter.3
  116.1 86.8 all-reduce.2
  205.4 21.9 reduce-scatter.5
  235.5 86.8 all-reduce.4
  324.9 21.9 reduce-scatter.7
